TPU v7x, 256 devices: a whole 4x4x8 slice. The times are simulated.
256 devices in a mesh: layer: 32 (over y, z_lo, core), batch: 8 (over x, z_hi).
Axes of the slice: x: 4, y: 4, z: 8 (z_hi: 2, z_lo: 4; z = z_hi * 4 + z_lo), core: 2. Of those that a mesh axis runs over, the one named last changes fastest.
Arguments:
- u_c: bfloat16 [32, 64, 32, 32, 128], P('layer', 'batch'), may hold values from -6 to 6
- lam_c: bfloat16 [32, 64, 32, 32, 128], P('layer', 'batch'), may hold values from -6 to 6
- weights: bfloat16 [64, 3, 3, 128, 128], P('layer'), may hold values from -0.1875 to 0.1875
Outputs:
- lam_low: bfloat16 [32, 64, 32, 32, 128], P('layer', 'batch')
- weight_grad: float32 [64, 3, 3, 128, 128], P('layer')
All inputs are finite; a program needn't handle non-finite values.
Results may differ from a plain program's by a relative error of at most 0.02.
Values may be sent and summed in bfloat16 or wider, within the bound.
A program may use at most 64 MiB of HBM per device.

v0:
```python
import functools

import jax
import jax.numpy as jnp
from jax import lax
from jax.experimental import pallas as pl
from jax.experimental.pallas import tpu as pltpu
from jax.sharding import PartitionSpec as P

f32 = jnp.float32
bf16 = jnp.bfloat16
MESH = pl.DeviceIdType.MESH
IMAGES = 8
PAIRS = 16
ROWS = 8
CHUNKS = tuple(range(0, PAIRS, ROWS))
W = 32
C = 128
K = 3 * C
CHUNK = 288
PIECES = 2
PIECE = CHUNK // PIECES
TAPS = (((0, 0, 0), (0, 1, 1)), ((0, 1, 0), (1, 0, 1)), ((1, 0, 0), (1, 1, 1)))
depth_step = 0.5


def silu_parts(v):
    t = 0.5 * jnp.tanh(0.5 * v) + 0.5
    return v * t, depth_step * (t * (1.0 + v * (1.0 - t)))


def put_rows(x_ref, at, parity, value):
    column = lax.broadcasted_iota(jnp.int32, value.shape, 1)
    before = jnp.where(column == 0, 0.0, pltpu.roll(value, 1, 1))
    after = jnp.where(column == W - 1, 0.0, pltpu.roll(value, W - 1, 1))
    first = at if parity == 0 else at + 1
    lane = K if parity == 0 else 0
    for b, part in enumerate((before, value, after)):
        x_ref[first : first + ROWS, :, lane + b * C : lane + (b + 1) * C] = part.astype(bf16)


def clear_edges(x_ref):
    x_ref[0, :, 0:K] = jnp.zeros((W, K), bf16)
    x_ref[PAIRS, :, K : 2 * K] = jnp.zeros((W, K), bf16)


def conv(x_ref, w_ref, at):
    n = ROWS // 2 * W
    d = x_ref[at : at + ROWS].reshape(ROWS // 2, 2, W, 2 * K)
    later = x_ref[at + 1 : at + ROWS + 1].reshape(ROWS // 2, 2, W, 2 * K)
    d0, d1, d2 = (v.reshape(n, 2 * K) for v in (d[:, 0], d[:, 1], later[:, 1]))
    shared = jnp.dot(d1, w_ref[1], preferred_element_type=f32)
    upper = shared + jnp.dot(d0 - d1, w_ref[0], preferred_element_type=f32)
    lower = shared + jnp.dot(d2 - d1, w_ref[2], preferred_element_type=f32)
    shape = (ROWS // 2, W, 2 * C)
    y = jnp.stack([upper.reshape(shape), lower.reshape(shape)], axis=1).reshape(ROWS, W, 2 * C)
    return y[:, :, :C], y[:, :, C:]


def fill_weights(dst, src, layer, transposed):
    for t in range(2):
        for q in range(2):
            for p in range(2):
                a = 2 * t + q - p
                for b in range(3):
                    rows = slice(q * K + b * C, q * K + (b + 1) * C)
                    cols = slice(p * C, (p + 1) * C)
                    if not 0 <= a <= 2:
                        dst[2 * t, rows, cols] = jnp.zeros((C, C), bf16)
                    elif transposed:
                        dst[2 * t, rows, cols] = src[layer, 2 - a, 2 - b].T
                    else:
                        dst[2 * t, rows, cols] = src[layer, a, b]
    dst[1] = dst[0] + dst[2]


def kernel(
    u_hbm, lam_hbm, w_hbm, low_v, summed,
    u_v, lam_v, w_v, xs0, xs1, xq, xr, g0, g1, bottom, top, a1, acc,
    wf, wt0, wt1, part, rs_buf, z_own, z_buf, gathered,
    u_sem, lam_sem, w_sem, send_sem, recv_sem,
    rs_send, rs_recv, z_send, z_recv, ag_send, ag_recv,
):
    layer = lax.axis_index("layer")
    batch = lax.axis_index("batch")
    x, zh = batch // 2, batch % 2
    below, above = jnp.maximum(layer - 1, 0), jnp.minimum(layer + 1, 31)
    has_below, has_above = layer > 0, layer < 31
    over_links = layer % 2 == 1

    def at_x(d):
        return (layer, ((x + d) % 4) * 2 + zh)

    twin = (layer, x * 2 + 1 - zh)

    def w_copy(slot):
        return pltpu.make_async_copy(w_hbm.at[slot], w_v.at[slot], w_sem.at[slot])

    def u_copy(i):
        return pltpu.make_async_copy(u_hbm.at[i], u_v.at[i], u_sem.at[i])

    def lam_copy(i):
        return pltpu.make_async_copy(lam_hbm.at[i], lam_v.at[i], lam_sem.at[i])

    u_copy(0).start()
    w_copy(0).start()
    lam_copy(0).start()
    w_copy(1).start()
    barrier = pltpu.get_barrier_semaphore()

    @pl.when(has_below)
    def _():
        pl.semaphore_signal(barrier, inc=1, device_id=(below, batch), device_id_type=MESH)

    @pl.when(has_above)
    def _():
        pl.semaphore_signal(barrier, inc=1, device_id=(above, batch), device_id_type=MESH)

    for d in (1, 2, 3):
        pl.semaphore_signal(barrier, inc=1, device_id=at_x(d), device_id_type=MESH)
    pl.semaphore_signal(barrier, inc=1, device_id=twin, device_id_type=MESH)

    clear_edges(xq.at[0])
    clear_edges(xq.at[1])
    clear_edges(xr)
    acc[...] = jnp.zeros_like(acc)

    def clear(i, carry):
        clear_edges(xs0.at[i])
        clear_edges(xs1.at[i])
        return carry

    lax.fori_loop(0, IMAGES, clear, 0)
    def send_copy(i):
        return pltpu.make_async_remote_copy(
            src_ref=bottom.at[i], dst_ref=top.at[i], send_sem=send_sem.at[i], recv_sem=recv_sem.at[i],
            device_id=(below, batch), device_id_type=MESH,
        )

    def lanes(p):
        return slice(p * C, (p + 1) * C)

    def load(i):
        u_copy(i).wait()
        lam_copy(i).wait()

    def open_state(i, slot, at):
        rows = slice(at, at + ROWS)
        for p in range(2):
            s, g = silu_parts(u_v[i, rows, p].astype(f32))
            put_rows(xs0.at[i], at, p, s)
            g0[slot, rows, :, lanes(p)] = g.astype(bf16)

    def open_adjoint(i, slot, at):
        for p in range(2):
            put_rows(xq.at[slot], at, p, lam_v[i, at : at + ROWS, p].astype(f32))

    def first_pass(i, carry):
        now, then = lax.rem(i, 2), lax.rem(i + 1, 2)
        ahead = jnp.minimum(i + 1, IMAGES - 1)

        @pl.when(i < IMAGES - 1)
        def _():
            load(ahead)

        for at in CHUNKS:
            rows = slice(at, at + ROWS)
            for p, y in enumerate(conv(xs0.at[i], wf, at)):
                moved = (u_v[i, rows, p].astype(f32) + depth_step * y).astype(bf16).astype(f32)
                s, g = silu_parts(moved)
                put_rows(xs1.at[i], at, p, s)
                g1[i, rows, :, lanes(p)] = g.astype(bf16)
        for at in CHUNKS:
            rows = slice(at, at + ROWS)
            for p, y in enumerate(conv(xq.at[now], wt1, at)):
                g = g1[i, rows, :, lanes(p)].astype(f32)
                put_rows(xr, at, p, (lam_v[i, rows, p].astype(f32) + g * y).astype(bf16).astype(f32))
            open_adjoint(ahead, then, at)
        for at in CHUNKS:
            rows = slice(at, at + ROWS)
            for p, y in enumerate(conv(xr, wt0, at)):
                first, lane = (at, K + C) if p == 0 else (at + 1, C)
                centre = xr[first : first + ROWS, :, lane : lane + C].astype(f32)
                g = g0[now, rows, :, lanes(p)].astype(f32)
                bottom[i, rows, :, lanes(p)] = (centre + g * y).astype(bf16)
            open_state(ahead, then, at)

        @pl.when(has_below)
        def _():
            send_copy(i).start()

        @pl.when(jnp.logical_not(has_above))
        def _():
            for p in range(2):
                top[i, :, :, lanes(p)] = lam_v[i, :, p]

        return carry

    u_copy(0).wait()
    for at in CHUNKS:
        open_state(0, 0, at)
    lam_copy(0).wait()
    w_copy(0).wait()
    w_copy(1).wait()
    for i in range(1, IMAGES):
        u_copy(i).start()
        lam_copy(i).start()
    fill_weights(wf, w_v, 0, False)
    for at in CHUNKS:
        open_adjoint(0, 0, at)
    fill_weights(wt1, w_v, 1, True)
    fill_weights(wt0, w_v, 0, True)
    peers = 4 + jnp.where(has_below, 1, 0) + jnp.where(has_above, 1, 0)
    pl.semaphore_wait(barrier, peers)

    lax.fori_loop(0, IMAGES, first_pass, 0)

    def add_grad(slot, xs, adj, i, count):
        n = count * PAIRS // 2 * W
        r = adj[pl.ds(i, count)].reshape(count, PAIRS // 2, 2, W, 2 * C)
        d = xs[pl.ds(i, count), 0:PAIRS].reshape(count, PAIRS // 2, 2, W, 2 * K)
        later = xs[pl.ds(i, count), 1 : PAIRS + 1].reshape(count, PAIRS // 2, 2, W, 2 * K)
        r0, r1 = r[:, :, 0], r[:, :, 1]
        d0, d1, d2 = d[:, :, 0], d[:, :, 1], later[:, :, 1]
        for t, (left, right) in enumerate(((d0 - d1, r0), (d1, r0 + r1), (d2 - d1, r1))):
            acc[slot, t] += lax.dot_general(
                left.reshape(n, 2 * K), right.reshape(n, 2 * C),
                (((0,), (0,)), ((), ())), preferred_element_type=f32,
            )

    def step_back(i, slot):
        for at in CHUNKS:
            rows = slice(at, at + ROWS)
            for p in range(2):
                put_rows(xq.at[slot], at, p, top[i, rows, :, lanes(p)].astype(f32))
        for at in CHUNKS:
            rows = slice(at, at + ROWS)
            for p, y in enumerate(conv(xq.at[slot], wt1, at)):
                moved = top[i, rows, :, lanes(p)].astype(f32) + g1[i, rows, :, lanes(p)].astype(f32) * y
                a1[i, rows, :, lanes(p)] = moved.astype(bf16)
                low_v[i, rows, p] = moved.astype(bf16)

    def arrived(i):
        @pl.when(has_above)
        def _():
            send_copy(i).wait_recv()

    def second_pass(j, carry):
        for slot in range(2):
            arrived(2 * j + slot)
            step_back(2 * j + slot, slot)
        add_grad(1, xs1, top, 2 * j, 2)

        @pl.when(jnp.logical_or(j < 2, over_links))
        def _():
            add_grad(0, xs0, a1, 2 * j, 2)

        return carry

    factor = depth_step / (IMAGES * 8)

    def piece(k, first=0):
        return pl.ds(pl.multiple_of(first + k * PIECE, 16), PIECE)

    def rs_copy(slot, k, d):
        to = (x + d) % 4
        return pltpu.make_async_remote_copy(
            src_ref=part.at[slot, piece(k, to * CHUNK)], dst_ref=rs_buf.at[slot, d - 1, piece(k)],
            send_sem=rs_send.at[slot, k, d - 1], recv_sem=rs_recv.at[slot, k, d - 1],
            device_id=at_x(d), device_id_type=MESH,
        )

    def z_copy(slot, k):
        return pltpu.make_async_remote_copy(
            src_ref=z_own.at[slot, piece(k)], dst_ref=z_buf.at[slot, piece(k)],
            send_sem=z_send.at[slot, k], recv_sem=z_recv.at[slot, k],
            device_id=twin, device_id_type=MESH,
        )

    def ag_copy(slot, k, d):
        return pltpu.make_async_remote_copy(
            src_ref=gathered.at[slot, x, piece(k)], dst_ref=gathered.at[slot, x, piece(k)],
            send_sem=ag_send.at[slot, k, d - 1], recv_sem=ag_recv.at[slot, k, d - 1],
            device_id=at_x(d), device_id_type=MESH,
        )

    def scatter(slot):
        for a, terms in enumerate(TAPS):
            total = 0.0
            for t, q, p in terms:
                block = (slice(q * K, (q + 1) * K), lanes(p))
                total += acc[slot, t, *block] + acc[slot, t + 1, *block]
            part[slot, a * K : (a + 1) * K] = (factor * total).astype(bf16)
        for k in range(PIECES):
            for d in (2, 1, 3):
                rs_copy(slot, k, d).start()

    def exchange(slot, k):
        for d in (1, 3, 2):
            rs_copy(slot, k, d).wait_recv()
        total = part[slot, piece(k, x * CHUNK)].astype(f32)
        for d in (1, 2, 3):
            total += rs_buf[slot, d - 1, piece(k)].astype(f32)
        z_own[slot, piece(k)] = total.astype(bf16)
        z_copy(slot, k).start()

    def gather(slot, k):
        z_copy(slot, k).wait_recv()
        total = z_own[slot, piece(k)].astype(f32) + z_buf[slot, piece(k)].astype(f32)
        gathered[slot, x, piece(k)] = total.astype(bf16)
        for d in (2, 1, 3):
            ag_copy(slot, k, d).start()

    def finish(slot):
        for k in range(PIECES):
            for d in (1, 3, 2):
                ag_copy(slot, k, d).wait_recv()
        summed[slot] = gathered[slot]

    lax.fori_loop(0, IMAGES // 2 - 1, second_pass, 0)
    arrived(IMAGES - 2)
    add_grad(1, xs1, top, IMAGES - 2, 1)
    step_back(IMAGES - 2, 0)

    @pl.when(over_links)
    def _():
        add_grad(0, xs0, a1, IMAGES - 2, 1)

    arrived(IMAGES - 1)
    add_grad(1, xs1, top, IMAGES - 1, 1)
    scatter(1)
    step_back(IMAGES - 1, 1)

    @pl.when(over_links)
    def _():
        add_grad(0, xs0, a1, IMAGES - 1, 1)

    @pl.when(jnp.logical_not(over_links))
    def _():
        add_grad(0, xs0, a1, IMAGES - 4, 4)

    scatter(0)
    order = [(slot, k) for slot in (1, 0) for k in range(PIECES)]
    for slot, k in order:
        exchange(slot, k)
    for slot, k in order:
        gather(slot, k)
    finish(1)
    finish(0)

    for slot in range(2):
        for k in range(PIECES):
            for d in (1, 2, 3):
                rs_copy(slot, k, d).wait_send()
                ag_copy(slot, k, d).wait_send()
            z_copy(slot, k).wait_send()

    def drain(i, carry):
        @pl.when(has_below)
        def _():
            send_copy(i).wait_send()

        return carry

    lax.fori_loop(0, IMAGES, drain, 0)


def deliver(low_v, sum_v, low_out, grad_out, grad_v, low_sem, grad_sem):
    def low_copy(i):
        return pltpu.make_async_copy(low_v.at[i], low_out.at[i], low_sem.at[i])

    def grad_copy(slot):
        return pltpu.make_async_copy(grad_v.at[slot], grad_out.at[slot], grad_sem.at[slot])

    for i in range(IMAGES):
        low_copy(i).start()
    for slot in range(2):
        grad_v[slot] = sum_v[slot].astype(f32)
        grad_copy(slot).start()
    for slot in range(2):
        grad_copy(slot).wait()
    for i in range(IMAGES):
        low_copy(i).wait()


def body(u_c, lam_c, weights):
    image = (IMAGES, PAIRS, 2, W, C)
    pair = (IMAGES, PAIRS, W, 2 * C)
    patch = (PAIRS + 1, W, 2 * K)
    wide = (3, 2 * K, 2 * C)
    vmem, dma = pltpu.VMEM, pltpu.SemaphoreType.DMA
    low, grad = pl.pallas_call(
        kernel,
        out_shape=(pltpu.VMEM(image, bf16), pltpu.VMEM((2, 4, CHUNK, C), bf16)),
        in_specs=[pl.BlockSpec(memory_space=pl.ANY)] * 3,
        out_specs=(pl.BlockSpec(memory_space=vmem),) * 2,
        scratch_shapes=[
            vmem(image, bf16), vmem(image, bf16), vmem((2, 3, 3, C, C), bf16),
            vmem((IMAGES,) + patch, bf16), vmem((IMAGES,) + patch, bf16), vmem((2,) + patch, bf16), vmem(patch, bf16),
            vmem((2, PAIRS, W, 2 * C), bf16), vmem(pair, bf16),
            vmem(pair, bf16), vmem(pair, bf16), vmem(pair, bf16),
            vmem((2, 3, 2 * K, 2 * C), f32),
            vmem(wide, bf16), vmem(wide, bf16), vmem(wide, bf16),
            vmem((2, 9 * C, C), bf16), vmem((2, 3, CHUNK, C), bf16),
            vmem((2, CHUNK, C), bf16), vmem((2, CHUNK, C), bf16),
            vmem((2, 4, CHUNK, C), bf16),
            dma((IMAGES,)), dma((IMAGES,)), dma((2,)),
            dma((IMAGES,)), dma((IMAGES,)),
            dma((2, PIECES, 3)), dma((2, PIECES, 3)), dma((2, PIECES)), dma((2, PIECES)),
            dma((2, PIECES, 3)), dma((2, PIECES, 3)),
        ],
        compiler_params=pltpu.CompilerParams(
            collective_id=0, has_side_effects=True, vmem_limit_bytes=52 * 2**20
        ),
        cost_estimate=pl.CostEstimate(flops=15 * 10**9, bytes_accessed=10**7, transcendentals=2 * 10**6),
        name="relax",
    )(u_c.reshape(image), lam_c.reshape(image), weights)
    low, grad = pl.pallas_call(
        deliver,
        out_shape=(
            jax.ShapeDtypeStruct(image, bf16),
            jax.ShapeDtypeStruct((2, 4, CHUNK, C), f32),
        ),
        in_specs=[pl.BlockSpec(memory_space=vmem)] * 2,
        out_specs=(pl.BlockSpec(memory_space=pl.ANY),) * 2,
        scratch_shapes=[vmem((2, 4, CHUNK, C), f32), dma((IMAGES,)), dma((2,))],
        compiler_params=pltpu.CompilerParams(vmem_limit_bytes=8 * 2**20),
        name="deliver",
    )(low, grad)
    return low.reshape(1, IMAGES, 2 * PAIRS, W, C), grad.reshape(2, 3, 3, C, C)


def solution(mesh):
    placed = (
        P("layer", "batch", None, None, None),
        P("layer", "batch", None, None, None),
        P("layer", None, None, None, None),
    )
    return jax.shard_map(
        body,
        mesh=mesh,
        in_specs=placed,
        out_specs=(P("layer", "batch", None, None, None), P("layer", None, None, None, None)),
        check_vma=False,
    )
```

profile of v0, /device:TPU:1, one launch (start us, length us, event | category | flops | bytes accessed | tf_op | source)
XLA Modules:
  0.0 56.4 jit_solution(6949832113582718698)
XLA Ops:
  0.6 54.0 %relax.1 = (bf16[8,16,2,32,128]{4,3,2,1,0:T(8,128)(2,1)S(1)}, bf16[2,4,288,128]{3,2,1,0:T(8,128)(2,1)S(1)}) custom-call(bf16[8,16,2,32,128]{4,3,2,1,0:T(8,128)(2,1)} %bitcast.4, bf16[8,16,2,32,128]{4,3,2,1,0:T(8,128)(2,1)} %bitcast.5, bf16[2,3,3,128,128]{4,3,2,1,0:T(8,128)(2,1)} %w_hbm.1), custom_call_target="tpu_custom_call" | custom-call | flops 15000000512 | bytes 10000000 | tf_op jit(solution)/shard_map/relax/pallas_call | solution.py:392
  54.6 1.8 %deliver.1 = (bf16[8,16,2,32,128]{4,3,2,1,0:T(8,128)(2,1)}, f32[2,4,288,128]{3,2,1,0:T(8,128)}) custom-call(bf16[8,16,2,32,128]{4,3,2,1,0:T(8,128)(2,1)S(1)} %get-tuple-element.6.low_v, bf16[2,4,288,128]{3,2,1,0:T(8,128)(2,1)S(1)} %get-tuple-element.7.sum_v), custom_call_target="tpu_custom_call" | custom-call | tf_op jit(solution)/shard_map/deliver/pallas_call | solution.py:418
where the time goes:
time: 56.5 us; the launch traced here: 56.4 us
  Pallas kernels  55.8 us (99%)
  between operations  0.64 us (1%)
    pallas_call x1, Pallas kernels, body(): pl.pallas_call(kernel, out_shape=(pltpu.VMEM(image, bf16), pltpu.VMEM((2,...  54 us
    pallas_call x1, Pallas kernels, body(): pl.pallas_call(deliver, out_shape=(jax.ShapeDtypeStruct(image, bf16), jax...  1.8 us

commit v1 on v0

--- a/solution.py
+++ b/solution.py
@@ -18,7 +18,7 @@
 C = 128
 K = 3 * C
 CHUNK = 288
-PIECES = 2
+PIECES = 3
 PIECE = CHUNK // PIECES
 TAPS = (((0, 0, 0), (0, 1, 1)), ((0, 1, 0), (1, 0, 1)), ((1, 0, 0), (1, 1, 1)))
 depth_step = 0.5
@@ -251,7 +251,7 @@
             step_back(2 * j + slot, slot)
         add_grad(1, xs1, top, 2 * j, 2)
 
-        @pl.when(jnp.logical_or(j < 2, over_links))
+        @pl.when(over_links)
         def _():
             add_grad(0, xs0, a1, 2 * j, 2)
 
@@ -337,6 +337,7 @@
 
     @pl.when(jnp.logical_not(over_links))
     def _():
+        add_grad(0, xs0, a1, 0, 4)
         add_grad(0, xs0, a1, IMAGES - 4, 4)
 
     scatter(0)

time: 56.5 us -> 55.9 us (0.989)
  Pallas kernels: 55.8 us -> 55 us
    pallas_call x1, Pallas kernels: 54 us -> 53.2 us  [body(): pl.pallas_call(kernel, out_shape=(pltpu.VMEM(image, bf16), pltpu.VMEM((2,...]
where the time goes in v1:
time: 55.9 us; the launch traced here: 55.8 us
  Pallas kernels  55 us (98%)
  between operations  0.8 us (1%)
    pallas_call x1, Pallas kernels, body(): pl.pallas_call(kernel, out_shape=(pltpu.VMEM(image, bf16), pltpu.VMEM((2,...  53.2 us
    pallas_call x1, Pallas kernels, body(): pl.pallas_call(deliver, out_shape=(jax.ShapeDtypeStruct(image, bf16), jax...  1.8 us

profile of v1, /device:TPU:1, one launch (start us, length us, event | category | flops | bytes accessed | tf_op | source)
XLA Modules:
  0.0 55.8 jit_solution(12431020877526023593)
XLA Ops:
  0.6 53.2 %relax.1 = (bf16[8,16,2,32,128]{4,3,2,1,0:T(8,128)(2,1)S(1)}, bf16[2,4,288,128]{3,2,1,0:T(8,128)(2,1)S(1)}) custom-call(bf16[8,16,2,32,128]{4,3,2,1,0:T(8,128)(2,1)} %bitcast.4, bf16[8,16,2,32,128]{4,3,2,1,0:T(8,128)(2,1)} %bitcast.5, bf16[2,3,3,128,128]{4,3,2,1,0:T(8,128)(2,1)} %w_hbm.1), custom_call_target="tpu_custom_call" | custom-call | flops 15000000512 | bytes 10000000 | tf_op jit(solution)/shard_map/relax/pallas_call | solution.py:393
  53.9 1.8 %deliver.1 = (bf16[8,16,2,32,128]{4,3,2,1,0:T(8,128)(2,1)}, f32[2,4,288,128]{3,2,1,0:T(8,128)}) custom-call(bf16[8,16,2,32,128]{4,3,2,1,0:T(8,128)(2,1)S(1)} %get-tuple-element.6.low_v, bf16[2,4,288,128]{3,2,1,0:T(8,128)(2,1)S(1)} %get-tuple-element.7.sum_v), custom_call_target="tpu_custom_call" | custom-call | tf_op jit(solution)/shard_map/deliver/pallas_call | solution.py:419
